TPU v7x, 32 devices: a whole 2x2x4 slice. The times are simulated.
32 devices in a mesh: ctx: 16 (over z, x, core), exp: 2 (over y).
Axes of the slice: x: 2, y: 2, z: 4, core: 2. Of those that a mesh axis runs over, the one named last changes fastest.
Arguments:
- hidden_acts: bfloat16 [32, 16, 32, 2048], P('ctx', None, None, 'exp'), may hold values from -6 to 6
- down_weight: bfloat16 [32, 2048, 2880], P('ctx', 'exp'), may hold values from -0.125 to 0.125
- expert_ids: int32 [2048, 4], P('ctx'), may hold values from 0 to 31, all different within a row; in each aligned block of 128 rows (0 to 127, 128 to 255, ...) at most 32 rows name the same one
- route_logits: float32 [2048, 4], P('ctx'), may hold values from -4 to 4
- out_grad: bfloat16 [2048, 2880], P('ctx', 'exp'), may hold values from -6 to 6
Outputs:
- combined: bfloat16 [2048, 2880], P('ctx', 'exp')
- grad_logits: float32 [2048, 4], P('ctx')
- grad_hidden: bfloat16 [32, 16, 32, 2048], P('ctx', None, None, 'exp')
- grad_weight: bfloat16 [32, 2048, 2880], P('ctx', 'exp')
Inputs may be any that keep to these rules, and one draw needn't show every extreme that they name: `expert_ids`: each token names 4 different experts; within each aligned block of 128 tokens no expert is named by more than 32 tokens, a bound that some block reaches.
All inputs are finite; a program needn't handle non-finite values.
Results may differ from a plain program's by a relative error of at most 0.014.
Values may be sent and summed in bfloat16 or wider, within the bound.
A program may use at most 128 MiB of HBM per device.

v0:
```python
import jax
import jax.numpy as jnp
from jax import lax
from jax.sharding import PartitionSpec as P


def slot_index(group_ids, expert_count):
    onehot = (group_ids[..., None] == jnp.arange(expert_count, dtype=jnp.int32)).astype(jnp.int32)
    running = jnp.cumsum(onehot, axis=1)
    return jnp.sum(running * onehot, axis=2) - 1


def local(hidden_acts, down_weight, expert_ids, route_logits, out_grad):
    ctx_count = lax.axis_size("ctx")
    local_experts = hidden_acts.shape[0]
    capacity = hidden_acts.shape[2]
    tok_rows = expert_ids.shape[0]
    top_count = expert_ids.shape[1]
    all_experts = local_experts * ctx_count
    weights = jnp.exp(route_logits)
    route_probs = weights / jnp.sum(weights, axis=1, keepdims=True)
    slot_pos = slot_index(expert_ids.reshape(1, -1), all_experts).reshape(-1)
    flat_index = expert_ids.reshape(-1) * capacity + slot_pos
    partial_value = jnp.einsum(
        "escj,ejd->escd", hidden_acts, down_weight, preferred_element_type=jnp.float32
    ).astype(jnp.bfloat16)
    returned = lax.all_to_all(partial_value, "ctx", split_axis=1, concat_axis=0, tiled=True)
    width = returned.shape[3]
    picked = (
        returned.reshape(all_experts * capacity, width)[flat_index]
        .reshape(tok_rows, top_count, width)
        .astype(jnp.float32)
    )
    mixed_rows = jnp.einsum("tk,tkd->td", route_probs, picked)
    combined = lax.psum_scatter(mixed_rows, "exp", scatter_dimension=1, tiled=True).astype(
        jnp.bfloat16
    )
    full_grad = lax.all_gather(out_grad, "exp", axis=1, tiled=True).astype(jnp.float32)
    prob_part = jnp.einsum("td,tkd->tk", full_grad, picked)
    slot_rows = (
        (route_probs[:, :, None] * full_grad[:, None, :]).astype(jnp.bfloat16).reshape(-1, width)
    )
    grad_table = (
        jnp.zeros((all_experts * capacity, width), jnp.bfloat16).at[flat_index].set(slot_rows)
    )
    slot_grad = lax.all_to_all(
        grad_table.reshape(all_experts, 1, capacity, width),
        "ctx",
        split_axis=0,
        concat_axis=1,
        tiled=True,
    )
    prob_grad = lax.psum(prob_part, "exp")
    grad_logits = route_probs * (
        prob_grad - jnp.sum(route_probs * prob_grad, axis=1, keepdims=True)
    )
    grad_hidden = jnp.einsum(
        "escd,ejd->escj", slot_grad, down_weight, preferred_element_type=jnp.float32
    ).astype(jnp.bfloat16)
    grad_weight = jnp.einsum(
        "escj,escd->ejd", hidden_acts, slot_grad, preferred_element_type=jnp.float32
    ).astype(jnp.bfloat16)
    return (combined, grad_logits, grad_hidden, grad_weight)


def solution(mesh):
    placed = (
        P("ctx", None, None, "exp"),
        P("ctx", "exp", None),
        P("ctx", None),
        P("ctx", None),
        P("ctx", "exp"),
    )
    return jax.shard_map(
        local,
        mesh=mesh,
        in_specs=placed,
        out_specs=(
            P("ctx", "exp"),
            P("ctx", None),
            P("ctx", None, None, "exp"),
            P("ctx", "exp", None),
        ),
        check_vma=False,
    )
```

profile of v0, /device:TPU:15, one launch (start us, length us, event | category | flops | bytes accessed | tf_op | source)
XLA Modules:
  0.0 370.6 jit_solution(7837871362400039301)
XLA Ops:
  7.2 1.6 copy-done
  8.8 12.9 %fusion.8 = bf16[2,16,32,2880]{3,2,1,0:T(8,128)(2,1)} fusion(bf16[2,16,32,1024]{3,2,1,0:T(8,128)(2,1)S(1)} %copy-done, bf16[2,1024,2880]{1,2,0:T(8,128)(2,1)} %param.6), kind=kOutput, calls=%fused_computation.14 | convolution fusion | flops 6042746880 | bytes 19791872 | tf_op jit(solution)/shard_map/escj,ejd->escd/dot_general | solution.py:24
  21.7 6.0 %copy.19 = bf16[2,16,32,2880]{3,2,0,1:T(8,128)(2,1)} copy(bf16[2,16,32,2880]{3,2,1,0:T(8,128)(2,1)} %fusion.8) | data formatting | bytes 11796480 | tf_op jit(solution)/shard_map/convert_element_type | solution.py:26
  27.6 6.7 %all-to-all-start = ((bf16[2,16,32,2880]{3,2,0,1:T(8,128)(2,1)}), bf16[2,16,32,2880]{3,2,0,1:T(8,128)(2,1)}, u32[]{:S(2)}, u32[]{:S(2)}) async-start(bf16[2,16,32,2880]{3,2,0,1:T(8,128)(2,1)} %copy.19), calls=%async_computation | async-start | bytes 12058624 | tf_op jit(solution)/shard_map/all_to_all | solution.py:27
  34.3 0.1 copy.21
  34.4 0.1 copy.20
  34.7 0.1 eq.27
  34.8 1.2 reduce-window.6
  36.1 0.2 slice_reduce_fusion
  36.4 10.8 %all_gather.3 = bf16[128,2880]{0,1:T(8,128)(2,1)S(1)} all-gather(bf16[128,1440]{0,1:T(8,128)(2,1)S(1)} %copy-done.1), channel_id=1, replica_groups=mesh['ctx'=16,'exp'=2] {'exp'}, dimensions={1}, use_global_device_ids=true | all-gather | bytes 1105920 | tf_op jit(solution)/shard_map/all_gather | solution.py:38
  47.2 1.4 copy.48
  48.6 5.0 %mul.51 = f32[128,4,2880]{2,1,0:T(4,128)} broadcast(f32[128,2880]{1,0:T(8,128)} %copy.48), dimensions={0,2} | broadcast | bytes 7372800 | tf_op jit(solution)/shard_map/mul | solution.py:41
  53.6 7.8 %mul.52 = f32[512,2880]{1,0:T(8,128)} reshape(f32[128,4,2880]{2,1,0:T(4,128)} %mul.51) | data formatting | bytes 11796480 | tf_op jit(solution)/shard_map/mul | solution.py:41
  61.5 0.1 fusion.19
  61.7 104.4 %all-to-all-done = bf16[2,16,32,2880]{3,2,0,1:T(8,128)(2,1)} async-done(((bf16[2,16,32,2880]{3,2,0,1:T(8,128)(2,1)}), bf16[2,16,32,2880]{3,2,0,1:T(8,128)(2,1)}, u32[]{:S(2)}, u32[]{:S(2)}) %all-to-all-start) | async-done | bytes 5898272 | tf_op jit(solution)/shard_map/all_to_all | solution.py:27
  166.1 10.2 %gather_fusion = bf16[512,2880]{1,0:T(8,128)(2,1)} fusion(bf16[1024,2880]{1,0:T(8,128)(2,1)} %bitcast.5, s32[1024]{0:T(1024)S(1)} %pad_clamp_fusion), kind=kCustom, calls=%fused_computation | custom fusion | bytes 5900288 | tf_op jit(solution)/shard_map/gather | solution.py:30
  176.3 5.9 %reshape.187 = bf16[128,4,2880]{2,1,0:T(4,128)(2,1)} reshape(bf16[512,2880]{1,0:T(8,128)(2,1)} %gather_fusion) | data formatting | bytes 5898240 | tf_op jit(solution)/shard_map/reshape | solution.py:31
  182.2 4.0 %multiply_reduce_fusion = f32[128,4]{1,0:T(8,128)S(1)} fusion(f32[128,2880]{1,0:T(8,128)} %copy.48, bf16[128,4,2880]{2,1,0:T(4,128)(2,1)} %reshape.187), kind=kLoop, calls=%fused_computation.10 | loop fusion | flops 4423168 | bytes 4425728
  186.2 4.0 %psum.7 = f32[128,4]{0,1:T(4,128)S(1)} all-reduce(f32[128,4]{0,1:T(4,128)S(1)} %copy.39), channel_id=1, replica_groups=mesh['ctx'=16,'exp'=2] {'exp'}, use_global_device_ids=true, to_apply=%region_5.6 | all-reduce | flops 512 | bytes 4096 | tf_op jit(solution)/shard_map/psum | solution.py:53
  190.2 0.1 copy.47
  190.4 0.1 mul.49
  190.5 10.5 %scatter_custom_fusion = bf16[1024,2880]{1,0:T(8,128)(2,1)} fusion(s32[512]{0:T(512)S(1)} %bitcast.58, f32[512,2880]{1,0:T(8,128)} %mul.52, f32[512]{0:T(512)S(1)} %mul.49, bf16[]{:T(256)} %constant.17.clone.1), kind=kCustom, calls=%fused_computation.15 | custom fusion | flops 2949120 | bytes 11798530 | tf_op jit(solution)/shard_map/scatter | solution.py:44
  201.0 6.1 %all-to-all-start.1 = ((bf16[32,1,32,2880]{3,2,1,0:T(8,128)(2,1)}), bf16[32,1,32,2880]{3,2,1,0:T(8,128)(2,1)}, u32[]{:S(2)}, u32[]{:S(2)}) async-start(bf16[32,1,32,2880]{3,2,1,0:T(8,128)(2,1)} %bitcast.53), calls=%async_computation.2 | async-start | bytes 12058624 | tf_op jit(solution)/shard_map/all_to_all | solution.py:46
  207.1 0.3 reduce-scatter.2.cloned.1.call-start
  207.4 7.2 %multiply_reduce_fusion.1 = f32[128,2880]{1,0:T(8,128)} fusion(bf16[128,4,2880]{2,1,0:T(4,128)(2,1)} %reshape.187, f32[128,4]{1,0:T(8,128)S(1)} %copy.47), kind=kLoop, calls=%fused_computation.11 | loop fusion | flops 4055040 | bytes 4425728
  214.6 3.0 copy.34
  217.6 0.6 subtract_multiply_fusion
  218.2 24.2 %reduce-scatter.2.cloned.1.call-done = f32[128,1440]{0,1:T(8,128)} async-done(((f32[128,2880]{0,1:T(8,128)}), f32[128,1440]{0,1:T(8,128)}) %reduce-scatter.2.cloned.1.call-update) | async-done | bytes 737296 | tf_op jit(solution)/shard_map/reduce_scatter | solution.py:35
  242.4 1.9 convert_element_type.33
  244.3 94.5 %all-to-all-done.1 = bf16[32,1,32,2880]{3,2,1,0:T(8,128)(2,1)} async-done(((bf16[32,1,32,2880]{3,2,1,0:T(8,128)(2,1)}), bf16[32,1,32,2880]{3,2,1,0:T(8,128)(2,1)}, u32[]{:S(2)}, u32[]{:S(2)}) %all-to-all-start.1) | async-done | bytes 5898272 | tf_op jit(solution)/shard_map/all_to_all | solution.py:46
  338.9 13.1 %fusion.14 = bf16[2,16,32,1024]{3,2,1,0:T(8,128)(2,1)} fusion(bf16[2,1024,2880]{1,2,0:T(8,128)(2,1)} %param.6, bf16[16,2,1,32,2880]{4,3,1,0,2:T(8,128)(2,1)} %bitcast.15), kind=kOutput, calls=%fused_computation.18 | convolution fusion | flops 6040846336 | bytes 19791872 | tf_op jit(solution)/shard_map/escd,ejd->escj/dot_general | solution.py:57
  351.9 11.8 %fusion = bf16[2,1024,2880]{1,2,0:T(8,128)(2,1)} fusion(bf16[2,16,32,1024]{3,2,1,0:T(8,128)(2,1)S(1)} %copy-done, bf16[2,16,32,2880]{3,2,0,1:T(8,128)(2,1)} %bitcast.20), kind=kOutput, calls=%fused_computation.3 | convolution fusion | flops 6045696000 | bytes 19791872 | tf_op jit(solution)/shard_map/escj,escd->ejd/dot_general | solution.py:60
  (23 shorter events, 0.6 us)
Async XLA Ops:
  7.2 1.6 copy-start
  27.6 6.7 %copy-start.3 = (s32[128,4]{0,1:T(4,128)S(1)}, s32[128,4]{0,1:T(4,128)}, u32[]{:S(2)}) copy-start(s32[128,4]{0,1:T(4,128)} %param.7) | copy-start | bytes 6148
  27.6 8.8 %copy-start.1 = (bf16[128,1440]{0,1:T(8,128)(2,1)S(1)}, bf16[128,1440]{0,1:T(8,128)(2,1)}, u32[]{:S(2)}) copy-start(bf16[128,1440]{0,1:T(8,128)(2,1)} %param.9) | copy-start | bytes 1105924
  27.6 138.5 %all-to-all-start = ((bf16[2,16,32,2880]{3,2,0,1:T(8,128)(2,1)}), bf16[2,16,32,2880]{3,2,0,1:T(8,128)(2,1)}, u32[]{:S(2)}, u32[]{:S(2)}) async-start(bf16[2,16,32,2880]{3,2,0,1:T(8,128)(2,1)} %copy.19), calls=%async_computation | async-start | bytes 12058624 | tf_op jit(solution)/shard_map/all_to_all | solution.py:27
  53.6 7.8 %copy-start.2 = (f32[128,4]{0,1:T(4,128)S(1)}, f32[128,4]{0,1:T(4,128)}, u32[]{:S(2)}) copy-start(f32[128,4]{0,1:T(4,128)} %param.8) | copy-start | bytes 6148
  201.0 137.8 %all-to-all-start.1 = ((bf16[32,1,32,2880]{3,2,1,0:T(8,128)(2,1)}), bf16[32,1,32,2880]{3,2,1,0:T(8,128)(2,1)}, u32[]{:S(2)}, u32[]{:S(2)}) async-start(bf16[32,1,32,2880]{3,2,1,0:T(8,128)(2,1)} %bitcast.53), calls=%async_computation.2 | async-start | bytes 12058624 | tf_op jit(solution)/shard_map/all_to_all | solution.py:46
  207.1 35.4 %reduce-scatter.2.cloned.1.call-start = ((), (), s32[]{:S(2)}) async-start(), calls=%async_computation.3 | async-start | bytes 2211840 | tf_op jit(solution)/shard_map/reduce_scatter | solution.py:35
Sparse Core Ops, SparseCore 0:
  217.8 24.6 reduce-scatter.1
where the time goes:
time: 372 us; the launch traced here: 371 us
  waiting for transfers between devices  223 us (60%)
  local copies, waits for them, and re-layouts  42 us (11%)
  matrix products  37.8 us (10%)
  other arithmetic  25.7 us (7%)
  blocking collectives  14.8 us (4%)
  between operations  14.1 us (4%)
  starting transfers between devices  13 us (3%)
    all_to_all x1, waiting for transfers between devices, local(): lax.all_to_all(partial_value, 'ctx', split_axis=1, concat_axis=0, tiled=T...  104 us
    all_to_all x1, waiting for transfers between devices, local(): lax.all_to_all(grad_table.reshape(all_experts, 1, capacity, width), 'ctx'...  94.5 us
    reduce_scatter x1, waiting for transfers between devices, local(): lax.psum_scatter(mixed_rows, 'exp', scatter_dimension=1, tiled=True)  24.2 us
    dot_general x1, matrix products, local(): jnp.einsum('escd,ejd->escj', slot_grad, down_weight, preferred_element_ty...  13.1 us
    mul x3, local copies, waits for them, and re-layouts, local(): route_probs[:, :, None] * full_grad[:, None, :]  12.9 us
    dot_general x1, matrix products, local(): jnp.einsum('escj,ejd->escd', hidden_acts, down_weight, preferred_element_...  12.9 us
    dot_general x1, matrix products, local(): jnp.einsum('escj,escd->ejd', hidden_acts, slot_grad, preferred_element_ty...  11.8 us
    unnamed x2, other arithmetic  11.2 us
  transfers between devices with their start and end apart: 3, of which 3 were waited for; matrix products, arithmetic and copies ran while one was open for 8% of the time, Pallas kernels for 0%

commit v1 on v0

v1 whole, which is shorter than its diff:
```python
import jax
import jax.numpy as jnp
from jax import lax
from jax.sharding import PartitionSpec as P

AXES = ("ctx", "exp")


def local(hidden_acts, down_weight, expert_ids, route_logits, out_grad):
    local_experts, groups, capacity, _ = hidden_acts.shape
    tok_rows, top_count = expert_ids.shape
    width = out_grad.shape[1]
    parts = lax.axis_size("exp")
    first = lax.axis_index("ctx") * local_experts

    weights = jnp.exp(route_logits)
    route_probs = weights / jnp.sum(weights, axis=1, keepdims=True)

    full_grad = lax.all_gather(out_grad, AXES).reshape(groups, parts, tok_rows, width)
    routes = lax.all_gather(
        jnp.concatenate([expert_ids.astype(jnp.float32), route_probs], axis=1).T, "ctx"
    )
    ids = routes[:, :top_count].astype(jnp.int32)
    probs = routes[:, top_count:]

    mine = first + jnp.arange(local_experts, dtype=jnp.int32)
    named = ids[None] == mine[:, None, None, None]
    taken = jnp.any(named, axis=2)
    prob_of = jnp.sum(jnp.where(named, probs[None], 0.0), axis=2)
    order = jnp.arange(tok_rows)
    earlier = (order[:, None] < order[None, :]).astype(jnp.bfloat16)
    position = jnp.einsum(
        "ect,tu->ecu", taken.astype(jnp.bfloat16), earlier, preferred_element_type=jnp.float32
    ).astype(jnp.int32)
    slots = jnp.arange(capacity, dtype=jnp.int32)
    holds = taken[:, :, None, :] & (position[:, :, None, :] == slots[:, None])
    select = holds.astype(jnp.bfloat16)
    slot_prob = jnp.sum(jnp.where(holds, prob_of[:, :, None, :], 0.0), axis=3)

    rows = (
        jnp.einsum(
            "escj,ejd->escd", hidden_acts, down_weight, preferred_element_type=jnp.float32
        )
        * slot_prob[..., None]
    ).astype(jnp.bfloat16)
    mixed = jnp.stack(
        [
            jnp.einsum(
                "ecst,ecsd->ctd",
                select,
                rows[..., part * width : (part + 1) * width],
                preferred_element_type=jnp.float32,
            ).astype(jnp.bfloat16)
            for part in range(parts)
        ],
        axis=1,
    )
    combined = lax.psum_scatter(
        mixed.reshape(groups * parts, tok_rows, width), AXES, scatter_dimension=0
    )

    slot_grad = jnp.concatenate(
        [
            (
                jnp.einsum(
                    "ecst,ctd->ecsd",
                    select,
                    full_grad[:, part],
                    preferred_element_type=jnp.float32,
                )
                * slot_prob[..., None]
            ).astype(jnp.bfloat16)
            for part in range(parts)
        ],
        axis=3,
    )
    grad_acts = jnp.einsum(
        "escd,ejd->escj", slot_grad, down_weight, preferred_element_type=jnp.float32
    )
    grad_hidden = grad_acts.astype(jnp.bfloat16)
    slot_sum = jnp.sum(grad_acts * hidden_acts.astype(jnp.float32), axis=3)
    token_sum = jnp.sum(jnp.where(holds, slot_sum[..., None], 0.0), axis=2)
    route_sum = jnp.sum(jnp.where(named, token_sum[:, :, None, :], 0.0), axis=0)
    route_sum = lax.psum(lax.psum_scatter(route_sum, "ctx", scatter_dimension=0), "exp").T
    grad_logits = route_sum - route_probs * jnp.sum(route_sum, axis=1, keepdims=True)
    grad_weight = jnp.einsum(
        "escj,escd->ejd", hidden_acts, slot_grad, preferred_element_type=jnp.float32
    ).astype(jnp.bfloat16)
    return (combined, grad_logits, grad_hidden, grad_weight)


def solution(mesh):
    placed = (
        P("ctx", None, None, "exp"),
        P("ctx", "exp", None),
        P("ctx", None),
        P("ctx", None),
        P("ctx", "exp"),
    )
    return jax.shard_map(
        local,
        mesh=mesh,
        in_specs=placed,
        out_specs=(
            P("ctx", "exp"),
            P("ctx", None),
            P("ctx", None, None, "exp"),
            P("ctx", "exp", None),
        ),
        check_vma=False,
    )
```

time: 372 us -> 298 us (0.80)
  the two profiles are of different devices: /device:TPU:15 before, /device:TPU:0 now
where the time goes in v1:
time: 298 us
  blocking collectives  89.5 us (30%)
  waiting for transfers between devices  68.3 us (23%)
  local copies, waits for them, and re-layouts  60.4 us (20%)
  matrix products  60.3 us (20%)
  between operations  14.2 us (5%)
  other arithmetic  4.68 us (2%)
    all_gather x1, waiting for transfers between devices, local(): lax.all_gather(out_grad, AXES).reshape(groups, parts, tok_rows, width)  67.6 us
    unnamed x1, blocking collectives  61.2 us
    reshape x1, local copies, waits for them, and re-layouts, local(): lax.all_gather(out_grad, AXES).reshape(groups, parts, tok_rows, width)  27.1 us
    slice x1, local copies, waits for them, and re-layouts, local(): full_grad[:, part]  23.7 us
    all_gather x1, blocking collectives, local(): lax.all_gather(jnp.concatenate([expert_ids.astype(jnp.float32), route_pro...  23.3 us
    dot_general x2, matrix products, local(): jnp.einsum('ecst,ctd->ecsd', select, full_grad[:, part], preferred_elemen...  16.2 us
    dot_general x1, matrix products, local(): jnp.einsum('escj,escd->ejd', hidden_acts, slot_grad, preferred_element_ty...  15.9 us
    dot_general x1, matrix products, local(): jnp.einsum('escd,ejd->escj', slot_grad, down_weight, preferred_element_ty...  11.9 us
  transfers between devices with their start and end apart: 2, of which 1 were waited for; matrix products, arithmetic and copies ran while one was open for 42% of the time, Pallas kernels for 0%

profile of v1, /device:TPU:0, one launch (start us, length us, event | category | flops | bytes accessed | tf_op | source)
XLA Modules:
  0.0 297.5 jit_solution(5130411791740159750)
XLA Ops:
  7.2 0.0 all-gather.4.cloned.1.call-start
  7.2 0.7 all-gather.4.cloned.1.call-update
  7.9 0.0 reduce-scatter.2.cloned.1.call-start
  7.9 0.7 convert_element_type.39
  8.6 0.7 exponential_reduce_fusion
  9.3 0.7 exponential_divide_fusion
  10.0 23.3 %all-gather = f32[128,128]{1,0:T(8,128)S(1)} all-gather(f32[8,128]{1,0:T(8,128)S(1)} %maximum_bitcast_fusion), channel_id=2, replica_groups=mesh['ctx'=16,'exp'=2] {'ctx'}, dimensions={0}, use_global_device_ids=true | all-gather | bytes 69632 | tf_op jit(solution)/shard_map/all_gather | solution.py:20
  33.4 0.1 fusion.30
  33.5 0.1 compare_reduce_fusion
  33.6 0.1 convolution_convert_fusion
  33.8 0.3 select_reduce_fusion.1
  34.0 11.8 %multiply_convert_fusion = bf16[2,16,32,2880]{3,2,1,0:T(8,128)(2,1)S(1)} fusion(f32[2,16,32]{2,1,0:T(8,128)S(1)} %copy.73, bf16[2,16,32,1024]{3,2,1,0:T(8,128)(2,1)} %param.5, bf16[2,1024,2880]{1,2,0:T(8,128)(2,1)} %param.6), kind=kOutput, calls=%fused_computation.1 | convolution fusion | flops 6045696000 | bytes 19795968 | tf_op jit(solution)/shard_map/escj,ejd->escd/dot_general | solution.py:41
  45.9 1.9 fusion.35
  47.7 2.2 fusion.13
  50.0 2.2 fusion.12
  52.2 1.2 pad_maximum_fusion
  53.4 5.7 %copy.76 = bf16[16,2,128,1440]{2,3,1,0:T(8,128)(2,1)} copy(bf16[16,2,128,1440]{2,3,0,1:T(8,128)(2,1)S(1)} %pad_maximum_fusion) | data formatting | bytes 23592960 | tf_op jit(solution)/shard_map/stack | solution.py:46
  59.2 0.6 copy-done.3
  59.8 0.6 dynamic-slice
  60.4 67.6 %all-gather.4.cloned.1.call-done = bf16[4096,1440]{0,1:T(8,128)(2,1)} async-done(((bf16[128,1440]{0,1:T(8,128)(2,1)}), bf16[4096,1440]{0,1:T(8,128)(2,1)}) %all-gather.4.cloned.1.call-update) | async-done | bytes 11796496 | tf_op jit(solution)/shard_map/all_gather | solution.py:19
  128.0 27.1 %reshape.29 = bf16[16,2,128,1440]{2,1,0,3:T(2,128)(2,1)} reshape(bf16[4096,1440]{0,1:T(8,128)(2,1)} %all-gather.4.cloned.1.call-done) | data formatting | bytes 23592960 | tf_op jit(solution)/shard_map/reshape | solution.py:19
  155.1 23.7 %fusion.34 = (bf16[16,1,128,1440]{2,1,0,3:T(2,128)(2,1)S(1)}, bf16[16,1,128,1440]{2,1,0,3:T(2,128)(2,1)}) fusion(bf16[16,2,128,1440]{2,1,0,3:T(2,128)(2,1)} %reshape.29), kind=kLoop, calls=%fused_computation.53 | loop fusion | bytes 23592960 | tf_op jit(solution)/shard_map/slice | solution.py:68
  178.8 10.2 %fusion.5 = bf16[2,16,32,1440]{3,2,0,1:T(8,128)(2,1)S(1)} fusion(bf16[16,1,128,1440]{2,1,0,3:T(2,128)(2,1)} %get-tuple-element.5, f32[2,16,32]{2,0,1:T(2,128)S(1)} %select_reduce_fusion.1, s32[2,16,128]{2,0,1:T(2,128)S(1)} %copy.70, pred[2,16,128]{2,0,1:T(4,128)(4,1)S(1)} %copy.69), kind=kOutput, calls=%fused_computation.11 | convolution fusion | flops 380698624 | bytes 8871936 | tf_op jit(solution)/shard_map/ecst,ctd->ecsd/dot_general | solution.py:65
  189.1 6.0 %fusion.6 = bf16[2,16,32,1440]{3,2,0,1:T(8,128)(2,1)S(1)} fusion(bf16[16,1,128,1440]{2,1,0,3:T(2,128)(2,1)S(1)} %get-tuple-element.4, f32[2,16,32]{2,0,1:T(2,128)S(1)} %select_reduce_fusion.1, s32[2,16,128]{2,0,1:T(2,128)S(1)} %copy.70, pred[2,16,128]{2,0,1:T(4,128)(4,1)S(1)} %copy.69), kind=kOutput, calls=%fused_computation.13 | convolution fusion | flops 380698624 | bytes 8871936 | tf_op jit(solution)/shard_map/ecst,ctd->ecsd/dot_general | solution.py:65
  195.1 11.9 %fusion.36 = (bf16[2,16,32,1024]{3,2,1,0:T(8,128)(2,1)}, f32[2,16,32]{2,1,0:T(8,128)S(1)}) fusion(bf16[2,16,32,1024]{3,2,1,0:T(8,128)(2,1)S(1)} %copy-done.2, bf16[2,1024,2880]{1,2,0:T(8,128)(2,1)} %param.6, bf16[2,16,32,1440]{3,2,0,1:T(8,128)(2,1)S(1)} %fusion.5, bf16[2,16,32,1440]{3,2,0,1:T(8,128)(2,1)S(1)} %fusion.6), kind=kOutput, calls=%fused_computation.55 | convolution fusion | flops 6055787520 | bytes 21893120 | tf_op jit(solution)/shard_map/escd,ejd->escj/dot_general | solution.py:77
  207.0 0.3 select_reduce_fusion
  207.3 0.1 fusion.31
  207.4 61.2 %all-reduce = f32[16,4,128]{2,1,0:T(4,128)S(1)} all-reduce(f32[16,4,128]{2,1,0:T(4,128)S(1)} %copy.82), channel_id=5, replica_groups=mesh['ctx'=16,'exp'=2] {'ctx'}, use_global_device_ids=true, to_apply=%region_8.9.clone | all-reduce | flops 8192 | bytes 65536
  268.6 0.6 dynamic-slice_bitcast_fusion
  269.3 4.9 %psum.7 = f32[4,128]{1,0:T(4,128)S(1)} all-reduce(f32[4,128]{1,0:T(4,128)S(1)} %dynamic-slice_bitcast_fusion), channel_id=1, replica_groups=mesh['ctx'=16,'exp'=2] {'exp'}, use_global_device_ids=true, to_apply=%region_9.10 | all-reduce | flops 512 | bytes 4096 | tf_op jit(solution)/shard_map/psum | solution.py:84
  274.2 0.6 bitcast_subtract_fusion
  274.8 15.9 %fusion = bf16[2,1024,2880]{1,2,0:T(8,128)(2,1)} fusion(bf16[2,16,32,1024]{3,2,1,0:T(8,128)(2,1)} %param.5, bf16[2,16,32,1440]{3,2,0,1:T(8,128)(2,1)S(1)} %fusion.5, bf16[2,16,32,1440]{3,2,0,1:T(8,128)(2,1)} %copy-done), kind=kOutput, calls=%fused_computation.2 | convolution fusion | flops 6057492480 | bytes 19791872 | tf_op jit(solution)/shard_map/escj,escd->ejd/dot_general | solution.py:86
  (22 shorter events, 0.2 us)
Async XLA Ops:
  7.2 120.8 %all-gather.4.cloned.1.call-start = ((), (), s32[]{:S(2)}) async-start(), calls=%async_computation.2 | async-start | bytes 12165120 | tf_op jit(solution)/shard_map/all_gather | solution.py:19
  7.9 282.8 %reduce-scatter.2.cloned.1.call-start = ((), (), s32[]{:S(2)}) async-start(), calls=%async_computation.1 | async-start | bytes 12165120 | tf_op jit(solution)/shard_map/reduce_scatter | solution.py:58
  59.1 0.7 copy-start.3
  189.1 6.0 %copy-start.2 = (bf16[2,16,32,1024]{3,2,1,0:T(8,128)(2,1)S(1)}, bf16[2,16,32,1024]{3,2,1,0:T(8,128)(2,1)}, u32[]{:S(2)}) copy-start(bf16[2,16,32,1024]{3,2,1,0:T(8,128)(2,1)} %param.5) | copy-start | bytes 6291460
  195.0 11.9 %copy-start = (bf16[2,16,32,1440]{3,2,0,1:T(8,128)(2,1)}, bf16[2,16,32,1440]{3,2,0,1:T(8,128)(2,1)S(1)}, u32[]{:S(2)}) copy-start(bf16[2,16,32,1440]{3,2,0,1:T(8,128)(2,1)S(1)} %fusion.6) | copy-start | bytes 8847364
  195.1 79.2 %copy-start.1 = (f32[128,4]{0,1:T(4,128)S(1)}, f32[128,4]{0,1:T(4,128)}, u32[]{:S(2)}) copy-start(f32[128,4]{0,1:T(4,128)} %param.8) | copy-start | bytes 6148
Sparse Core Ops, SparseCore 0:
  10.9 117.0 all-gather.3
  134.6 146.1 reduce-scatter.1

commit v2 on v1

v2 whole, which is shorter than its diff:
```python
import functools

import jax
import jax.numpy as jnp
from jax import lax
from jax.experimental import pallas as pl
from jax.experimental.pallas import tpu as pltpu
from jax.sharding import PartitionSpec as P

MESH = pl.DeviceIdType.MESH
PAIR = 2
F32 = jnp.float32
BF16 = jnp.bfloat16


def exchange_kernel(
    outer,
    parts,
    acts_ref,
    weight_ref,
    prob_ref,
    back_ref,
    grad_ref,
    full_ref,
    combined_ref,
    weight_v,
    rows_v,
    away_v,
    home_v,
    core_v,
    far0_v,
    far1_v,
    near0_v,
    near1_v,
    last_v,
    load_sem,
    az_s,
    az_r,
    au_s,
    au_r,
    av_s,
    av_r,
    ac_s,
    ac_r,
    rc_s,
    rc_r,
    rv_s,
    rv_r,
    ru_s,
    ru_r,
    rz_s,
    rz_r,
):
    ctx, y = lax.axis_index("ctx"), lax.axis_index("exp")
    z, x, c = ctx // (PAIR * PAIR), (ctx // PAIR) % PAIR, ctx % PAIR
    experts, capacity = rows_v.shape[1], rows_v.shape[2]
    tokens, width = grad_ref.shape
    half = tokens // 2
    spans = (pl.ds(0, half), pl.ds(half, half))

    def at_z(k):
        return (((z + k) % outer) * (PAIR * PAIR) + x * PAIR + c, y)

    def at_x(k):
        return (z * (PAIR * PAIR) + ((x + k) % PAIR) * PAIR + c, y)

    def at_y(k):
        return (ctx, (y + k) % parts)

    sibling = (z * (PAIR * PAIR) + x * PAIR + (1 - c), y)
    mid_to, mid_n = (at_x, at_y), (PAIR, parts)
    end_to, end_n = (at_y, at_x), (parts, PAIR)

    def send(src, dst, s, r, to):
        return pltpu.make_async_remote_copy(
            src_ref=src, dst_ref=dst, send_sem=s, recv_sem=r, device_id=to, device_id_type=MESH
        )

    loads = [
        pltpu.make_async_copy(weight_ref.at[e], weight_v.at[e], load_sem.at[e])
        for e in range(experts)
    ]
    for load in loads:
        load.start()
    own = pltpu.make_async_copy(grad_ref, full_ref.at[z, x, c, y], load_sem.at[experts])
    own.start()

    barrier = pltpu.get_barrier_semaphore()
    peers = [at_z(k) for k in range(1, outer)]
    peers += [at_x(k) for k in range(1, PAIR)]
    peers += [at_y(k) for k in range(1, parts)]
    peers += [sibling]
    for peer in peers:
        pl.semaphore_signal(barrier, inc=1, device_id=peer, device_id_type=MESH)
    pl.semaphore_wait(barrier, len(peers))

    def from_z(k):
        return (z - k + outer) % outer

    def gz(h, k):
        place = full_ref.at[z, x, c, y, spans[h]]
        return send(grad_ref.at[spans[h]], place, az_s.at[h, k], az_r.at[h, k], at_z(k))

    def gu(h, k, j):
        place = full_ref.at[from_z(k), x, c, y, spans[h]]
        return send(place, place, au_s.at[h, k, j], au_r.at[h, k, j], mid_to[h](j))

    def gv(h, k, j):
        if h == 0:
            place = full_ref.at[from_z(k), :, c, y, spans[h]]
        else:
            place = full_ref.at[from_z(k), x, c, :, spans[h]]
        return send(place, place, av_s.at[h, k, j], av_r.at[h, k, j], end_to[h](j))

    def gc(h, k):
        place = full_ref.at[from_z(k), :, c, :, spans[h]]
        return send(place, place, ac_s.at[h, k], ac_r.at[h, k], sibling)

    for k in range(1, outer):
        for h in range(2):
            gz(h, k).start()
    own.wait()

    def gather_mid(k):
        for h in range(2):
            if k:
                gz(h, k).wait_recv()
            for j in range(1, mid_n[h]):
                gu(h, k, j).start()

    def gather_end(k):
        for h in range(2):
            for j in range(1, mid_n[h]):
                gu(h, k, j).wait_recv()
            for j in range(1, end_n[h]):
                gv(h, k, j).start()

    def gather_core(k):
        for h in range(2):
            for j in range(1, end_n[h]):
                gv(h, k, j).wait_recv()
            gc(h, k).start()

    gather_mid(0)

    block = acts_ref.shape[1] // 2
    groups = block // capacity

    def product(e, m):
        start = pl.multiple_of(m * block, block)
        value = jnp.dot(
            acts_ref[e, pl.ds(start, block), :], weight_v[e], preferred_element_type=F32
        )
        value = (value * prob_ref[e, pl.ds(start, block), :]).astype(BF16)
        rows_v[pl.ds(m * groups, groups), e] = value.reshape(groups, capacity, value.shape[1])

    for e in range(experts):
        loads[e].wait()
        if e == 0:
            gather_end(0)
        else:
            for k in range(1, outer):
                gather_mid(k)
        lax.fori_loop(0, 2, lambda m, _: (product(e, m), 0)[1], 0)

    for k in range(1, outer):
        gather_end(k)

    order = list(range(1, outer)) + [0]

    def rc(i):
        zi = (z + order[i]) % outer
        return send(away_v.at[i % 2], core_v.at[zi], rc_s.at[i], rc_r.at[i], sibling)

    def rv(h, i, j):
        zi = (z + order[i]) % outer
        if h == 0:
            src, dst = home_v.at[zi, :, (y + j) % parts, spans[0]], far0_v.at[zi, j - 1]
        else:
            src, dst = home_v.at[zi, (x + j) % PAIR, :, spans[1]], far1_v.at[zi, j - 1]
        return send(src, dst, rv_s.at[h, i, j], rv_r.at[h, i, j], end_to[h](j))

    def ru(h, i, j):
        zi = (z + order[i]) % outer
        if h == 0:
            src, dst = far0_v.at[zi, 0, (x + j) % PAIR], near0_v.at[zi, j - 1]
        else:
            src, dst = far1_v.at[zi, 0, (y + j) % parts], near1_v.at[zi, j - 1]
        return send(src, dst, ru_s.at[h, i, j], ru_r.at[h, i, j], mid_to[h](j))

    near = (near0_v, near1_v)

    def rz(h, k):
        zi = (z + k) % outer
        return send(near[h].at[zi, 0], last_v.at[h, k - 1], rz_s.at[h, k], rz_r.at[h, k], at_z(k))

    def mix(zi, xi, ci, put):
        group = zi * (PAIR * PAIR) + xi * PAIR + ci
        value = jnp.dot(
            back_ref[group],
            rows_v[group].reshape(experts * capacity, rows_v.shape[3]),
            preferred_element_type=F32,
        ).astype(BF16)
        for part in range(parts):
            put(xi, part, value[:, part * width : (part + 1) * width])

    for i in range(outer):
        zi = (z + order[i]) % outer
        if i >= 2:
            rc(i - 2).wait_send()

        def put_away(xi, part, value):
            away_v[i % 2, xi, part] = value

        def put_home(xi, part, value):
            home_v[zi, xi, part] = value

        lax.fori_loop(0, PAIR, lambda xi, _: (mix(zi, xi, 1 - c, put_away), 0)[1], 0)
        rc(i).start()
        lax.fori_loop(0, PAIR, lambda xi, _: (mix(zi, xi, c, put_home), 0)[1], 0)
        gather_core(i)

    def add(first, others):
        total = first.astype(F32)
        for other in others:
            total = total + other.astype(F32)
        return total.astype(BF16)

    def sum_core(i):
        zi = (z + order[i]) % outer
        rc(i).wait_recv()

        def step(n, _):
            xi, part = n // parts, n % parts
            home_v[zi, xi, part] = add(home_v[zi, xi, part], [core_v[zi, xi, part]])
            return 0

        lax.fori_loop(0, PAIR * parts, step, 0)
        for h in range(2):
            for j in range(1, end_n[h]):
                rv(h, i, j).start()

    def sum_end(i):
        zi = (z + order[i]) % outer
        for h in range(2):
            for j in range(1, end_n[h]):
                rv(h, i, j).wait_recv()
        for xi in range(PAIR):
            others = [far0_v[zi, j - 1, xi] for j in range(1, end_n[0])]
            far0_v[zi, 0, xi] = add(home_v[zi, xi, y, spans[0]], others)
        for part in range(parts):
            others = [far1_v[zi, j - 1, part] for j in range(1, end_n[1])]
            far1_v[zi, 0, part] = add(home_v[zi, x, part, spans[1]], others)
        for h in range(2):
            for j in range(1, mid_n[h]):
                ru(h, i, j).start()

    def sum_mid(i):
        zi = (z + order[i]) % outer
        for h in range(2):
            for j in range(1, mid_n[h]):
                ru(h, i, j).wait_recv()
            others = [near[h][zi, j - 1] for j in range(1, mid_n[h])]
            mine = far0_v[zi, 0, x] if h == 0 else far1_v[zi, 0, y]
            near[h][zi, 0] = add(mine, others)
            if order[i]:
                rz(h, order[i]).start()

    sum_core(0)
    for i in range(outer):
        if i + 1 < outer:
            sum_core(i + 1)
        sum_end(i)
        if i:
            sum_mid(i - 1)
    sum_mid(outer - 1)

    for h in range(2):
        for k in range(1, outer):
            rz(h, k).wait_recv()
        combined_ref[spans[h], :] = add(
            near[h][z, 0], [last_v[h, k - 1] for k in range(1, outer)]
        )

    for h in range(2):
        for k in range(outer):
            if k:
                gz(h, k).wait_send()
                rz(h, k).wait_send()
            for j in range(1, mid_n[h]):
                gu(h, k, j).wait_send()
                ru(h, k, j).wait_send()
            for j in range(1, end_n[h]):
                gv(h, k, j).wait_send()
                rv(h, k, j).wait_send()
            gc(h, k).wait()
    for i in range(max(0, outer - 2), outer):
        rc(i).wait_send()


def exchange(acts, weight, slot_prob, back, out_grad, outer, parts):
    experts, slots, _ = acts.shape
    groups = outer * PAIR * PAIR
    capacity = slots // groups
    tokens, width = out_grad.shape
    full = parts * width
    half = tokens // 2
    vmem = pl.BlockSpec(memory_space=pltpu.VMEM)
    hbm = pl.BlockSpec(memory_space=pl.ANY)
    dma = pltpu.SemaphoreType.DMA
    most = max(PAIR, parts)
    pairs = [(2, outer), (2, outer, most), (2, outer, most), (2, outer)]
    pairs += [(outer,), (2, outer, most), (2, outer, most), (2, outer)]
    sems = [dma((experts + 1,))]
    for shape in pairs:
        sems += [dma(shape), dma(shape)]
    return pl.pallas_call(
        functools.partial(exchange_kernel, outer, parts),
        out_shape=(
            jax.ShapeDtypeStruct((outer, PAIR, PAIR, parts, tokens, width), BF16),
            jax.ShapeDtypeStruct((tokens, width), BF16),
        ),
        in_specs=[vmem, hbm, vmem, vmem, hbm],
        out_specs=(hbm, vmem),
        scratch_shapes=[
            pltpu.VMEM(weight.shape, BF16),
            pltpu.VMEM((groups, experts, capacity, full), BF16),
            pltpu.VMEM((2, PAIR, parts, tokens, width), BF16),
            pltpu.VMEM((outer, PAIR, parts, tokens, width), BF16),
            pltpu.VMEM((outer, PAIR, parts, tokens, width), BF16),
            pltpu.VMEM((outer, parts - 1, PAIR, half, width), BF16),
            pltpu.VMEM((outer, PAIR - 1, parts, half, width), BF16),
            pltpu.VMEM((outer, PAIR - 1, half, width), BF16),
            pltpu.VMEM((outer, parts - 1, half, width), BF16),
            pltpu.VMEM((2, outer - 1, half, width), BF16),
        ]
        + sems,
        compiler_params=pltpu.CompilerParams(
            collective_id=0, has_side_effects=True, vmem_limit_bytes=62 * 1024 * 1024
        ),
        cost_estimate=pl.CostEstimate(
            flops=2 * experts * slots * weight.shape[1] * full,
            bytes_accessed=4 * weight.size,
            transcendentals=0,
        ),
    )(acts, weight, slot_prob, back, out_grad)


def slots_kernel(select_ref, prob_ref, full_ref, out_ref):
    experts, _, capacity, _ = out_ref.shape
    parts, _, width = full_ref.shape[1:]
    for part in range(parts):
        value = jnp.dot(select_ref[0], full_ref[0, part], preferred_element_type=F32)
        value = (value * prob_ref[0]).astype(BF16).reshape(experts, capacity, width)
        out_ref[:, 0, :, part * width : (part + 1) * width] = value


def spread(select, slot_prob, full_grad, experts):
    groups, both, tokens = select.shape
    _, parts, _, width = full_grad.shape
    capacity = both // experts
    return pl.pallas_call(
        slots_kernel,
        grid=(groups,),
        out_shape=jax.ShapeDtypeStruct((experts, groups, capacity, parts * width), BF16),
        in_specs=[
            pl.BlockSpec((1, both, tokens), lambda g: (g, 0, 0)),
            pl.BlockSpec((1, both, 1), lambda g: (g, 0, 0)),
            pl.BlockSpec((1, parts, tokens, width), lambda g: (g, 0, 0, 0)),
        ],
        out_specs=pl.BlockSpec((experts, 1, capacity, parts * width), lambda g: (0, g, 0, 0)),
        compiler_params=pltpu.CompilerParams(vmem_limit_bytes=32 * 1024 * 1024),
    )(select, slot_prob, full_grad)


def local(hidden_acts, down_weight, expert_ids, route_logits, out_grad):
    local_experts, groups, capacity, hidden = hidden_acts.shape
    tok_rows, top_count = expert_ids.shape
    width = out_grad.shape[1]
    parts = lax.axis_size("exp")
    first = lax.axis_index("ctx") * local_experts

    weights = jnp.exp(route_logits)
    route_probs = weights / jnp.sum(weights, axis=1, keepdims=True)

    routes = lax.all_gather(
        jnp.concatenate([expert_ids.astype(F32), route_probs], axis=1).T, "ctx"
    )
    ids = routes[:, :top_count].astype(jnp.int32)
    probs = routes[:, top_count:]

    mine = first + jnp.arange(local_experts, dtype=jnp.int32)
    named = ids[:, None] == mine[None, :, None, None]
    taken = jnp.any(named, axis=2)
    prob_of = jnp.sum(jnp.where(named, probs[:, None], 0.0), axis=2)
    order = jnp.arange(tok_rows)
    earlier = (order[:, None] < order[None, :]).astype(BF16)
    position = jnp.einsum(
        "cet,tu->ceu", taken.astype(BF16), earlier, preferred_element_type=F32
    ).astype(jnp.int32)
    slots = jnp.arange(capacity, dtype=jnp.int32)
    holds = taken[:, :, None, :] & (position[:, :, None, :] == slots[:, None])
    slot_prob = jnp.sum(jnp.where(holds, prob_of[:, :, None, :], 0.0), axis=3)
    select = holds.astype(BF16).reshape(groups, local_experts * capacity, tok_rows)
    back = select.swapaxes(1, 2)

    full_grad, combined = exchange(
        hidden_acts.reshape(local_experts, groups * capacity, hidden),
        down_weight,
        slot_prob.swapaxes(0, 1).reshape(local_experts, groups * capacity, 1),
        back,
        out_grad,
        groups // (PAIR * PAIR),
        parts,
    )
    slot_grad = spread(
        select,
        slot_prob.reshape(groups, local_experts * capacity, 1),
        full_grad.reshape(groups, parts, tok_rows, width),
        local_experts,
    )
    grad_acts = jnp.einsum("escd,ejd->escj", slot_grad, down_weight, preferred_element_type=F32)
    grad_hidden = grad_acts.astype(BF16)
    slot_sum = jnp.sum(grad_acts * hidden_acts.astype(F32), axis=3).swapaxes(0, 1)
    token_sum = jnp.sum(jnp.where(holds, slot_sum[..., None], 0.0), axis=2)
    route_sum = jnp.sum(jnp.where(named, token_sum[:, :, None, :], 0.0), axis=1)
    route_sum = lax.psum(lax.psum_scatter(route_sum, "ctx", scatter_dimension=0), "exp").T
    grad_logits = route_sum - route_probs * jnp.sum(route_sum, axis=1, keepdims=True)
    grad_weight = jnp.einsum(
        "escj,escd->ejd", hidden_acts, slot_grad, preferred_element_type=F32
    ).astype(BF16)
    return (combined, grad_logits, grad_hidden, grad_weight)


def solution(mesh):
    placed = (
        P("ctx", None, None, "exp"),
        P("ctx", "exp", None),
        P("ctx", None),
        P("ctx", None),
        P("ctx", "exp"),
    )
    return jax.shard_map(
        local,
        mesh=mesh,
        in_specs=placed,
        out_specs=(
            P("ctx", "exp"),
            P("ctx", None),
            P("ctx", None, None, "exp"),
            P("ctx", "exp", None),
        ),
        check_vma=False,
    )
```

time: 298 us -> 285 us (0.956)
  Pallas kernels: 0 us -> 138 us
  waiting for transfers between devices: 68.3 us -> 0 us
  matrix products: 60.3 us -> 22.5 us
  local copies, waits for them, and re-layouts: 60.4 us -> 29.5 us
  between operations: 14.2 us -> 0.81 us
    pallas_call x0 -> x2, Pallas kernels: none -> 138 us  [the longest x1 133 us: exchange(): pl.pallas_call(functools.partial(exchange_kernel, outer, parts), out_shap...]
    all_gather x1 -> x0, waiting for transfers between devices: 67.6 us -> none  [local(): lax.all_gather(out_grad, AXES).reshape(groups, parts, tok_rows, width)]
    dot_general x6 -> x1, matrix products: 32.6 us -> 0.14 us  [local(): jnp.einsum('cet,tu->ceu', taken.astype(BF16), earlier, preferred_element_...]
    slice x2 -> x0, local copies, waits for them, and re-layouts: 25.6 us -> none  [the longest x1 23.7 us: local(): full_grad[:, part]]
    reshape x1 -> x2, local copies, waits for them, and re-layouts: 27.1 us -> 2.67 us  [the longest x1 1.33 us: local(): slot_prob.swapaxes(0, 1).reshape(local_experts, groups * capacity, 1)]
    unnamed x9 -> x28, local copies, waits for them, and re-layouts: 1.23 us -> 25 us
    another operation x1 -> x0, local copies, waits for them, and re-layouts: 5.75 us -> none  [local(): jnp.stack([jnp.einsum('ecst,ecsd->ctd', select, rows[..., part * width:(p...]
    dot_general x1, matrix products: 15.9 us -> 11.2 us  [local(): jnp.einsum('escj,escd->ejd', hidden_acts, slot_grad, preferred_element_ty...]
  transfers between devices with their start and end apart: 2 -> 0, of which waited for: 1 -> 0; matrix products, arithmetic and copies ran while one was open for 42% -> 0% of each run, Pallas kernels for 0% -> 0%
where the time goes in v2:
time: 285 us; the launch traced here: 284 us
  Pallas kernels  138 us (48%)
  blocking collectives  89.6 us (31%)
  local copies, waits for them, and re-layouts  29.5 us (10%)
  matrix products  22.5 us (8%)
  other arithmetic  3.66 us (1%)
    pallas_call x1, Pallas kernels, exchange(): pl.pallas_call(functools.partial(exchange_kernel, outer, parts), out_shap...  133 us
    unnamed x1, blocking collectives  61.5 us
    unnamed x28, local copies, waits for them, and re-layouts  25 us
    all_gather x1, blocking collectives, local(): lax.all_gather(jnp.concatenate([expert_ids.astype(F32), route_probs], axi...  23.2 us
    dot_general x1, matrix products, local(): jnp.einsum('escj,escd->ejd', hidden_acts, slot_grad, preferred_element_ty...  11.2 us
    dot_general x1, matrix products, local(): jnp.einsum('escd,ejd->escj', slot_grad, down_weight, preferred_element_ty...  11.1 us
    pallas_call x1, Pallas kernels, spread(): pl.pallas_call(slots_kernel, grid=(groups,), out_shape=jax.ShapeDtypeStru...  5.72 us

profile of v2, /device:TPU:0, one launch (start us, length us, event | category | flops | bytes accessed | tf_op | source)
XLA Modules:
  0.0 284.4 jit_solution(2190642346378426770)
XLA Ops:
  0.6 0.7 exponential_reduce_fusion
  1.3 0.5 copy-done.9
  1.8 0.7 exponential_divide_fusion
  2.5 0.7 convert_element_type.27
  3.2 23.2 %all-gather = f32[128,128]{1,0:T(8,128)S(1)} all-gather(f32[8,128]{1,0:T(8,128)S(1)} %maximum_bitcast_fusion), channel_id=2, replica_groups=mesh['ctx'=16,'exp'=2] {'ctx'}, dimensions={0}, use_global_device_ids=true | all-gather | bytes 69632 | tf_op jit(solution)/shard_map/all_gather | solution.py:386
  26.5 0.0 copy-start.7
  26.5 0.1 compare_reduce_fusion
  26.6 0.1 convolution_convert_fusion
  26.7 0.0 copy-start.4
  26.8 0.1 fusion.6
  26.9 0.3 select_reduce_fusion.1
  27.1 1.3 reshape.45.prob_ref
  28.5 0.1 eq.45
  28.6 0.2 fusion.5.select_ref
  28.7 1.0 copy.85.back_ref
  29.8 16.3 %copy.83.weight_ref = bf16[2,1024,2880]{2,1,0:T(8,128)(2,1)} copy(bf16[2,1024,2880]{1,2,0:T(8,128)(2,1)} %param.6) | data formatting | bytes 23592960 | tf_op args[1]
  46.1 1.0 copy.86.grad_ref
  47.1 132.6 %shard_map.84 = (bf16[4,2,2,2,128,1440]{5,4,3,2,1,0:T(8,128)(2,1)}, bf16[128,1440]{1,0:T(8,128)(2,1)}) custom-call(bf16[2,512,1024]{2,1,0:T(8,128)(2,1)} %bitcast.47, bf16[2,1024,2880]{2,1,0:T(8,128)(2,1)} %copy.83.weight_ref, f32[2,512,1]{2,1,0:T(8,128)} %reshape.45.prob_ref, bf16[16,128,64]{2,1,0:T(8,128)(2,1)} %copy.85.back_ref, ...), custom_call_target="tpu_custom_call" | custom-call | flops 6039797760 | bytes 23592960 | tf_op jit(solution)/shard_map/pallas_call | solution.py:317
  179.7 1.3 reshape.46.prob_ref
  181.1 4.6 %copy-done = bf16[4,2,2,2,128,1440]{5,4,3,2,1,0:T(8,128)(2,1)S(1)} copy-done((bf16[4,2,2,2,128,1440]{5,4,3,2,1,0:T(8,128)(2,1)S(1)}, bf16[4,2,2,2,128,1440]{5,4,3,2,1,0:T(8,128)(2,1)}, u32[]{:S(2)}) %copy-start) | copy-done | bytes 11796504
  185.6 1.0 copy-done.1
  186.7 5.7 %shard_map.85 = bf16[2,16,32,2880]{3,2,1,0:T(8,128)(2,1)S(1)} custom-call(bf16[16,64,128]{2,1,0:T(8,128)(2,1)S(1)} %fusion.5.select_ref, f32[16,64,1]{2,1,0:T(8,128)S(1)} %copy-done.1, bf16[16,2,128,1440]{3,2,1,0:T(8,128)(2,1)S(1)} %bitcast.42), custom_call_target="tpu_custom_call" | custom-call | tf_op jit(solution)/shard_map/pallas_call | solution.py:362
  192.4 11.2 %fusion = bf16[2,1024,2880]{1,2,0:T(8,128)(2,1)} fusion(bf16[2,16,32,2880]{3,2,1,0:T(8,128)(2,1)S(1)} %shard_map.85, bf16[2,16,32,1024]{3,2,1,0:T(8,128)(2,1)} %param.5), kind=kOutput, calls=%fused_computation.1 | convolution fusion | flops 6045696000 | bytes 19791872 | tf_op jit(solution)/shard_map/escj,escd->ejd/dot_general | solution.py:429
  203.7 11.1 %fusion.10 = (bf16[2,16,32,1024]{3,2,1,0:T(8,128)(2,1)}, f32[2,16,32]{2,1,0:T(8,128)S(1)}) fusion(bf16[2,16,32,1024]{3,2,1,0:T(8,128)(2,1)} %param.5, bf16[2,16,32,2880]{3,2,1,0:T(8,128)(2,1)S(1)} %shard_map.85, bf16[2,1024,2880]{1,2,0:T(8,128)(2,1)} %param.6), kind=kOutput, calls=%fused_computation.27 | convolution fusion | flops 6043991040 | bytes 21893120 | tf_op jit(solution)/shard_map/escd,ejd->escj/dot_general | solution.py:422
  214.8 0.3 select_reduce_fusion
  215.1 0.1 fusion.7
  215.2 61.5 %all-reduce = f32[16,4,128]{2,1,0:T(4,128)S(1)} all-reduce(f32[16,4,128]{2,1,0:T(4,128)S(1)} %copy.90), channel_id=3, replica_groups=mesh['ctx'=16,'exp'=2] {'ctx'}, use_global_device_ids=true, to_apply=%region_7.8.clone | all-reduce | flops 8192 | bytes 65536
  276.7 0.6 dynamic-slice
  277.3 0.6 dynamic-slice_bitcast_fusion
  277.9 4.9 %psum.7 = f32[4,128]{1,0:T(4,128)S(1)} all-reduce(f32[4,128]{1,0:T(4,128)S(1)} %dynamic-slice_bitcast_fusion), channel_id=1, replica_groups=mesh['ctx'=16,'exp'=2] {'exp'}, use_global_device_ids=true, to_apply=%region_8.9 | all-reduce | flops 512 | bytes 4096 | tf_op jit(solution)/shard_map/psum | solution.py:427
  282.9 0.6 bitcast_subtract_fusion
  283.5 0.9 copy.91
  (33 shorter events, 0.2 us)
Async XLA Ops:
  1.3 0.5 copy-start.9
  26.5 19.6 %copy-start.7 = (s32[2]{0:T(128)}, s32[2]{0:T(128)S(1)}, u32[]{:S(2)}) copy-start(s32[2]{0:T(128)S(1)} %iota_add_fusion) | copy-start | bytes 28
  26.7 2.0 copy-start.4
  29.8 16.4 %copy-start.3 = (bf16[128,1440]{0,1:T(8,128)(2,1)S(1)}, bf16[128,1440]{0,1:T(8,128)(2,1)}, u32[]{:S(2)}) copy-start(bf16[128,1440]{0,1:T(8,128)(2,1)} %param.9) | copy-start | bytes 1105924
  181.1 4.6 %copy-start = (bf16[4,2,2,2,128,1440]{5,4,3,2,1,0:T(8,128)(2,1)S(1)}, bf16[4,2,2,2,128,1440]{5,4,3,2,1,0:T(8,128)(2,1)}, u32[]{:S(2)}) copy-start(bf16[4,2,2,2,128,1440]{5,4,3,2,1,0:T(8,128)(2,1)} %get-tuple-element.7) | copy-start | bytes 35389444
  185.6 1.0 copy-start.1
  203.6 11.2 %copy-start.5 = (s32[16,2,128]{2,1,0:T(2,128)S(1)}, s32[16,2,128]{2,1,0:T(2,128)}, u32[]{:S(2)}) copy-start(s32[16,2,128]{2,1,0:T(2,128)} %copy-done.4) | copy-start | bytes 49156
  203.6 11.5 %copy-start.8 = (s32[2]{0:T(128)S(1)}, s32[2]{0:T(128)}, u32[]{:S(2)}) copy-start(s32[2]{0:T(128)} %copy-done.7) | copy-start | bytes 28
  203.6 73.1 %copy-start.11 = (u32[32]{0:T(128)S(1)}, u32[32]{0:T(128)}, u32[]{:S(2)}) copy-start(u32[32]{0:T(128)} %constant.16) | copy-start | bytes 388
  203.6 79.3 %copy-start.6 = (f32[128,4]{0,1:T(4,128)S(1)}, f32[128,4]{0,1:T(4,128)}, u32[]{:S(2)}) copy-start(f32[128,4]{0,1:T(4,128)} %param.8) | copy-start | bytes 6148
  203.7 79.3 %copy-start.10 = (f32[128]{0:T(128)S(1)}, f32[128]{0:T(128)}, u32[]{:S(2)}) copy-start(f32[128]{0:T(128)} %copy-done.9) | copy-start | bytes 1540
  203.7 79.8 %copy-start.2 = (bf16[128,1440]{1,0:T(8,128)(2,1)S(1)}, bf16[128,1440]{1,0:T(8,128)(2,1)}, u32[]{:S(2)}) copy-start(bf16[128,1440]{1,0:T(8,128)(2,1)} %get-tuple-element.32) | copy-start | bytes 1105924

commit v3 on v2

--- a/solution.py
+++ b/solution.py
@@ -20,9 +20,13 @@
     weight_ref,
     prob_ref,
     back_ref,
+    select_ref,
     grad_ref,
     full_ref,
     combined_ref,
+    hidden_ref,
+    slots_ref,
+    dots_ref,
     weight_v,
     rows_v,
     away_v,
@@ -34,6 +38,7 @@
     near1_v,
     last_v,
     load_sem,
+    fetch_sem,
     az_s,
     az_r,
     au_s,
@@ -148,10 +153,14 @@
 
     def product(e, m):
         start = pl.multiple_of(m * block, block)
-        value = jnp.dot(
-            acts_ref[e, pl.ds(start, block), :], weight_v[e], preferred_element_type=F32
+        value = lax.dot_general(
+            acts_ref[e, pl.ds(start, block), :],
+            weight_v[e],
+            (((1,), (1,)), ((), ())),
+            preferred_element_type=F32,
         )
-        value = (value * prob_ref[e, pl.ds(start, block), :]).astype(BF16)
+        prob = prob_ref[pl.ds(m * groups, groups), e].reshape(block, 1)
+        value = (value * prob).astype(BF16)
         rows_v[pl.ds(m * groups, groups), e] = value.reshape(groups, capacity, value.shape[1])
 
     for e in range(experts):
@@ -266,13 +275,66 @@
             if order[i]:
                 rz(h, order[i]).start()
 
-    sum_core(0)
     for i in range(outer):
-        if i + 1 < outer:
-            sum_core(i + 1)
+        sum_core(i)
+    for h in range(2):
+        for k in range(outer):
+            gc(h, k).wait_recv()
+
+    def fetch(i, ci):
+        zi = (z + order[i]) % outer
+        return pltpu.make_async_copy(full_ref.at[zi, :, ci], core_v.at[zi], fetch_sem.at[i, ci])
+
+    def spread(i, ci):
+        zi = (z + order[i]) % outer
+        fetch(i, ci).wait()
+
+        def step(xi, _):
+            group = zi * (PAIR * PAIR) + xi * PAIR + ci
+            prob = prob_ref[group].reshape(experts * capacity, 1)
+            for part in range(parts):
+                value = jnp.dot(
+                    select_ref[group], core_v[zi, xi, part], preferred_element_type=F32
+                )
+                rows_v[group, :, :, part * width : (part + 1) * width] = (
+                    (value * prob).astype(BF16).reshape(experts, capacity, width)
+                )
+            return 0
+
+        lax.fori_loop(0, PAIR, step, 0)
+
+    for i in range(outer):
+        fetch(i, 0).start()
+    for i in range(outer):
+        spread(i, 0)
+        fetch(i, 1).start()
         sum_end(i)
         if i:
             sum_mid(i - 1)
+    for i in range(outer):
+        spread(i, 1)
+    stores = [
+        pltpu.make_async_copy(rows_v.at[:, e], slots_ref.at[e], load_sem.at[e])
+        for e in range(experts)
+    ]
+    for store in stores:
+        store.start()
+
+    def pull(n, _):
+        e, m = n // 2, n % 2
+        start = pl.multiple_of(m * block, block)
+        value = jnp.dot(
+            rows_v[pl.ds(m * groups, groups), e].reshape(block, rows_v.shape[3]),
+            weight_v[e],
+            preferred_element_type=F32,
+        )
+        hidden_ref[e, pl.ds(start, block), :] = value.astype(BF16)
+        dots_ref[e, pl.ds(start, block), :] = jnp.sum(
+            value * acts_ref[e, pl.ds(start, block), :].astype(F32), axis=1, keepdims=True
+        )
+        return 0
+
+    lax.fori_loop(0, 2 * experts, pull, 0)
     sum_mid(outer - 1)
 
     for h in range(2):
@@ -293,12 +355,14 @@
             for j in range(1, end_n[h]):
                 gv(h, k, j).wait_send()
                 rv(h, k, j).wait_send()
-            gc(h, k).wait()
+            gc(h, k).wait_send()
     for i in range(max(0, outer - 2), outer):
         rc(i).wait_send()
-
-
-def exchange(acts, weight, slot_prob, back, out_grad, outer, parts):
+    for store in stores:
+        store.wait()
+
+
+def exchange(acts, weight, slot_prob, back, select, out_grad, outer, parts):
     experts, slots, _ = acts.shape
     groups = outer * PAIR * PAIR
     capacity = slots // groups
@@ -311,7 +375,7 @@
     most = max(PAIR, parts)
     pairs = [(2, outer), (2, outer, most), (2, outer, most), (2, outer)]
     pairs += [(outer,), (2, outer, most), (2, outer, most), (2, outer)]
-    sems = [dma((experts + 1,))]
+    sems = [dma((experts + 1,)), dma((outer, 2))]
     for shape in pairs:
         sems += [dma(shape), dma(shape)]
     return pl.pallas_call(
@@ -319,9 +383,12 @@
         out_shape=(
             jax.ShapeDtypeStruct((outer, PAIR, PAIR, parts, tokens, width), BF16),
             jax.ShapeDtypeStruct((tokens, width), BF16),
+            jax.ShapeDtypeStruct(acts.shape, BF16),
+            jax.ShapeDtypeStruct((experts, groups, capacity, full), BF16),
+            jax.ShapeDtypeStruct((experts, slots, 1), F32),
         ),
-        in_specs=[vmem, hbm, vmem, vmem, hbm],
-        out_specs=(hbm, vmem),
+        in_specs=[vmem, hbm, vmem, vmem, vmem, hbm],
+        out_specs=(hbm, vmem, vmem, hbm, vmem),
         scratch_shapes=[
             pltpu.VMEM(weight.shape, BF16),
             pltpu.VMEM((groups, experts, capacity, full), BF16),
@@ -339,38 +406,120 @@
             collective_id=0, has_side_effects=True, vmem_limit_bytes=62 * 1024 * 1024
         ),
         cost_estimate=pl.CostEstimate(
-            flops=2 * experts * slots * weight.shape[1] * full,
+            flops=4 * experts * slots * weight.shape[2] * full,
             bytes_accessed=4 * weight.size,
             transcendentals=0,
         ),
-    )(acts, weight, slot_prob, back, out_grad)
-
-
-def slots_kernel(select_ref, prob_ref, full_ref, out_ref):
-    experts, _, capacity, _ = out_ref.shape
-    parts, _, width = full_ref.shape[1:]
-    for part in range(parts):
-        value = jnp.dot(select_ref[0], full_ref[0, part], preferred_element_type=F32)
-        value = (value * prob_ref[0]).astype(BF16).reshape(experts, capacity, width)
-        out_ref[:, 0, :, part * width : (part + 1) * width] = value
-
-
-def spread(select, slot_prob, full_grad, experts):
-    groups, both, tokens = select.shape
-    _, parts, _, width = full_grad.shape
-    capacity = both // experts
+    )(acts, weight, slot_prob, back, select, out_grad)
+
+
+def routes_kernel(outer, mine_ref, all_ref, z_s, z_r, x_s, x_r, c_s, c_r):
+    ctx, y = lax.axis_index("ctx"), lax.axis_index("exp")
+    z, x, c = ctx // (PAIR * PAIR), (ctx // PAIR) % PAIR, ctx % PAIR
+    to_z = [(((z + k) % outer) * (PAIR * PAIR) + x * PAIR + c, y) for k in range(1, outer)]
+    to_x = (z * (PAIR * PAIR) + (1 - x) * PAIR + c, y)
+    to_c = (z * (PAIR * PAIR) + x * PAIR + (1 - c), y)
+    barrier = pltpu.get_barrier_semaphore()
+    for peer in to_z + [to_x, to_c]:
+        pl.semaphore_signal(barrier, inc=1, device_id=peer, device_id_type=MESH)
+    pl.semaphore_wait(barrier, outer + 1)
+
+    def send(src, dst, s, r, to):
+        copy = pltpu.make_async_remote_copy(
+            src_ref=src, dst_ref=dst, send_sem=s, recv_sem=r, device_id=to, device_id_type=MESH
+        )
+        copy.start()
+        return copy
+
+    place = all_ref.at[z, x, c]
+    along = [
+        send(mine_ref, place, z_s.at[k], z_r.at[k], peer) for k, peer in enumerate(to_z)
+    ]
+    all_ref[z, x, c] = mine_ref[...]
+    for copy in along:
+        copy.wait()
+    place = all_ref.at[:, x, c]
+    send(place, place, x_s, x_r, to_x).wait()
+    place = all_ref.at[:, :, c]
+    send(place, place, c_s, c_r, to_c).wait()
+
+
+def gather_routes(mine, outer):
+    vmem = pl.BlockSpec(memory_space=pltpu.VMEM)
+    dma = pltpu.SemaphoreType.DMA
     return pl.pallas_call(
-        slots_kernel,
-        grid=(groups,),
-        out_shape=jax.ShapeDtypeStruct((experts, groups, capacity, parts * width), BF16),
-        in_specs=[
-            pl.BlockSpec((1, both, tokens), lambda g: (g, 0, 0)),
-            pl.BlockSpec((1, both, 1), lambda g: (g, 0, 0)),
-            pl.BlockSpec((1, parts, tokens, width), lambda g: (g, 0, 0, 0)),
+        functools.partial(routes_kernel, outer),
+        out_shape=jax.ShapeDtypeStruct((outer, PAIR, PAIR) + mine.shape, mine.dtype),
+        in_specs=[vmem],
+        out_specs=vmem,
+        scratch_shapes=[dma((outer,)), dma((outer,)), dma, dma, dma, dma],
+        compiler_params=pltpu.CompilerParams(collective_id=1, has_side_effects=True),
+    )(mine)
+
+
+def total_kernel(
+    outer, parts, all_ref, out_ref, c_v, x_v, z_v, y_v, sum_c, sum_x,
+    c_s, c_r, x_s, x_r, z_s, z_r, y_s, y_r,
+):
+    ctx, y = lax.axis_index("ctx"), lax.axis_index("exp")
+    z, x, c = ctx // (PAIR * PAIR), (ctx // PAIR) % PAIR, ctx % PAIR
+    to_z = [(((z + k) % outer) * (PAIR * PAIR) + x * PAIR + c, y) for k in range(1, outer)]
+    to_y = [(ctx, (y + k) % parts) for k in range(1, parts)]
+    to_x = (z * (PAIR * PAIR) + (1 - x) * PAIR + c, y)
+    to_c = (z * (PAIR * PAIR) + x * PAIR + (1 - c), y)
+    barrier = pltpu.get_barrier_semaphore()
+    for peer in to_z + to_y + [to_x, to_c]:
+        pl.semaphore_signal(barrier, inc=1, device_id=peer, device_id_type=MESH)
+    pl.semaphore_wait(barrier, outer + parts)
+
+    def send(src, dst, s, r, to):
+        copy = pltpu.make_async_remote_copy(
+            src_ref=src, dst_ref=dst, send_sem=s, recv_sem=r, device_id=to, device_id_type=MESH
+        )
+        copy.start()
+        return copy
+
+    send(all_ref.at[:, :, 1 - c], c_v, c_s, c_r, to_c).wait()
+    sum_c[...] = all_ref[:, :, c] + c_v[...]
+    send(sum_c.at[:, 1 - x], x_v, x_s, x_r, to_x).wait()
+    sum_x[...] = sum_c[:, x] + x_v[...]
+    along = [
+        send(sum_x.at[(z + k) % outer], z_v.at[k - 1], z_s.at[k], z_r.at[k], to_z[k - 1])
+        for k in range(1, outer)
+    ]
+    for copy in along:
+        copy.wait()
+    total = sum_x[z]
+    for k in range(1, outer):
+        total = total + z_v[k - 1]
+    y_v[y] = total
+    place = y_v.at[y]
+    along = [send(place, place, y_s.at[k], y_r.at[k], to_y[k - 1]) for k in range(1, parts)]
+    for copy in along:
+        copy.wait()
+    out_ref[...] = jnp.sum(y_v[...], axis=0)
+
+
+def total_routes(values, outer, parts):
+    one = values.shape[3:]
+    vmem = pl.BlockSpec(memory_space=pltpu.VMEM)
+    dma = pltpu.SemaphoreType.DMA
+    return pl.pallas_call(
+        functools.partial(total_kernel, outer, parts),
+        out_shape=jax.ShapeDtypeStruct(one, F32),
+        in_specs=[vmem],
+        out_specs=vmem,
+        scratch_shapes=[
+            pltpu.VMEM((outer, PAIR) + one, F32),
+            pltpu.VMEM((outer,) + one, F32),
+            pltpu.VMEM((outer - 1,) + one, F32),
+            pltpu.VMEM((parts,) + one, F32),
+            pltpu.VMEM((outer, PAIR) + one, F32),
+            pltpu.VMEM((outer,) + one, F32),
+            dma, dma, dma, dma, dma((outer,)), dma((outer,)), dma((parts,)), dma((parts,)),
         ],
-        out_specs=pl.BlockSpec((experts, 1, capacity, parts * width), lambda g: (0, g, 0, 0)),
-        compiler_params=pltpu.CompilerParams(vmem_limit_bytes=32 * 1024 * 1024),
-    )(select, slot_prob, full_grad)
+        compiler_params=pltpu.CompilerParams(collective_id=2, has_side_effects=True),
+    )(values)
 
 
 def local(hidden_acts, down_weight, expert_ids, route_logits, out_grad):
@@ -383,9 +532,10 @@
     weights = jnp.exp(route_logits)
     route_probs = weights / jnp.sum(weights, axis=1, keepdims=True)
 
-    routes = lax.all_gather(
-        jnp.concatenate([expert_ids.astype(F32), route_probs], axis=1).T, "ctx"
-    )
+    outer = groups // (PAIR * PAIR)
+    routes = gather_routes(
+        jnp.concatenate([expert_ids.astype(F32), route_probs], axis=1).T, outer
+    ).reshape(groups, 2 * top_count, tok_rows)
     ids = routes[:, :top_count].astype(jnp.int32)
     probs = routes[:, top_count:]
 
@@ -404,27 +554,24 @@
     select = holds.astype(BF16).reshape(groups, local_experts * capacity, tok_rows)
     back = select.swapaxes(1, 2)
 
-    full_grad, combined = exchange(
+    _, combined, grad_hidden, slot_grad, slot_sum = exchange(
         hidden_acts.reshape(local_experts, groups * capacity, hidden),
-        down_weight,
-        slot_prob.swapaxes(0, 1).reshape(local_experts, groups * capacity, 1),
+        down_weight.swapaxes(1, 2),
+        slot_prob[..., None],
         back,
+        select,
         out_grad,
-        groups // (PAIR * PAIR),
+        outer,
         parts,
     )
-    slot_grad = spread(
-        select,
-        slot_prob.reshape(groups, local_experts * capacity, 1),
-        full_grad.reshape(groups, parts, tok_rows, width),
-        local_experts,
-    )
-    grad_acts = jnp.einsum("escd,ejd->escj", slot_grad, down_weight, preferred_element_type=F32)
-    grad_hidden = grad_acts.astype(BF16)
-    slot_sum = jnp.sum(grad_acts * hidden_acts.astype(F32), axis=3).swapaxes(0, 1)
+    grad_hidden = grad_hidden.reshape(hidden_acts.shape)
+    slot_sum = slot_sum.reshape(local_experts, groups, capacity).swapaxes(0, 1)
     token_sum = jnp.sum(jnp.where(holds, slot_sum[..., None], 0.0), axis=2)
     route_sum = jnp.sum(jnp.where(named, token_sum[:, :, None, :], 0.0), axis=1)
-    route_sum = lax.psum(lax.psum_scatter(route_sum, "ctx", scatter_dimension=0), "exp").T
+    route_sum = jnp.pad(route_sum, ((0, 0), (0, top_count), (0, 0)))
+    route_sum = total_routes(
+        route_sum.reshape(outer, PAIR, PAIR, 2 * top_count, tok_rows), outer, parts
+    )[:top_count].T
     grad_logits = route_sum - route_probs * jnp.sum(route_sum, axis=1, keepdims=True)
     grad_weight = jnp.einsum(
         "escj,escd->ejd", hidden_acts, slot_grad, preferred_element_type=F32

time: 285 us -> 208 us (0.73)
  blocking collectives: 89.6 us -> 0 us
  Pallas kernels: 138 us -> 178 us
  local copies, waits for them, and re-layouts: 29.5 us -> 9.14 us
  matrix products: 22.5 us -> 12.4 us
  other arithmetic: 3.66 us -> 6.85 us
    unnamed x1 -> x0, blocking collectives: 61.5 us -> none
    pallas_call x1 -> x2, Pallas kernels: 5.72 us -> 32.3 us  [the longest x1 19.5 us: total_routes(): pl.pallas_call(functools.partial(total_kernel, outer, parts), out_shape=j...]
    all_gather x1 -> x0, blocking collectives: 23.2 us -> none  [local(): lax.all_gather(jnp.concatenate([expert_ids.astype(F32), route_probs], axi...]
    unnamed x28 -> x10, local copies, waits for them, and re-layouts: 25 us -> 5.27 us
    pallas_call x1, Pallas kernels: 133 us -> 146 us  [exchange(): pl.pallas_call(functools.partial(exchange_kernel, outer, parts), out_shap...]
    dot_general x1 -> x0, matrix products: 11.1 us -> none  [local(): jnp.einsum('escd,ejd->escj', slot_grad, down_weight, preferred_element_ty...]
    psum x1 -> x0, blocking collectives: 4.94 us -> none  [local(): lax.psum(lax.psum_scatter(route_sum, 'ctx', scatter_dimension=0), 'exp')]
where the time goes in v3:
time: 208 us; the launch traced here: 207 us
  Pallas kernels  178 us (86%)
  matrix products  12.4 us (6%)
  local copies, waits for them, and re-layouts  9.14 us (4%)
  other arithmetic  6.85 us (3%)
    pallas_call x1, Pallas kernels, exchange(): pl.pallas_call(functools.partial(exchange_kernel, outer, parts), out_shap...  146 us
    pallas_call x1, Pallas kernels, total_routes(): pl.pallas_call(functools.partial(total_kernel, outer, parts), out_shape=j...  19.5 us
    pallas_call x1, Pallas kernels, gather_routes(): pl.pallas_call(functools.partial(routes_kernel, outer), out_shape=jax.Sha...  12.7 us
    dot_general x1, matrix products, local(): jnp.einsum('escj,escd->ejd', hidden_acts, slot_grad, preferred_element_ty...  12.2 us
    unnamed x10, local copies, waits for them, and re-layouts  5.27 us

profile of v3, /device:TPU:0, one launch (start us, length us, event | category | flops | bytes accessed | tf_op | source)
XLA Modules:
  0.0 207.3 jit_solution(2219391874518380909)
XLA Ops:
  0.6 0.7 exponential_reduce_fusion
  1.4 0.1 eq.45
  1.4 0.7 exponential_divide_fusion
  2.1 0.7 convert_element_type.23
  2.8 0.6 maximum_bitcast_fusion.mine_ref
  3.4 12.7 %shard_map.84 = f32[4,2,2,8,128]{4,3,2,1,0:T(8,128)} custom-call(f32[8,128]{1,0:T(8,128)} %maximum_bitcast_fusion.mine_ref), custom_call_target="tpu_custom_call" | custom-call | tf_op jit(solution)/shard_map/pallas_call | solution.py:450
  16.2 0.9 fusion.8
  17.1 0.1 compare_reduce_fusion
  17.2 0.1 convolution_convert_fusion
  17.4 0.1 fusion.4
  17.5 0.3 select_reduce_fusion.1
  17.7 0.2 fusion.3.select_ref
  17.9 0.0 copy-start.1
  17.9 2.0 copy.63.grad_ref
  19.9 1.1 copy.61.prob_ref
  21.0 1.0 copy.62.back_ref
  22.0 0.0 copy-done.1
  22.0 0.0 copy-start.2
  22.0 145.9 %shard_map.85 = (bf16[4,2,2,2,128,1440]{5,4,3,2,1,0:T(8,128)(2,1)}, bf16[128,1440]{1,0:T(8,128)(2,1)}, bf16[2,512,1024]{2,1,0:T(8,128)(2,1)}, bf16[2,16,32,2880]{3,2,1,0:T(8,128)(2,1)}, f32[2,512,1]{2,1,0:T(8,128)}) custom-call(bf16[2,512,1024]{2,1,0:T(8,128)(2,1)} %bitcast.40, bf16[2,2880,1024]{2,1,0:T(8,128)(2,1)} %bitcast.39, ...), custom_call_target="tpu_custom_call" | custom-call | flops 12079595520 | bytes 23592960 | tf_op jit(solution)/shard_map/pallas_call | solution.py:381
  167.9 1.9 copy.67
  169.8 1.2 reduce.1
  171.1 0.1 reshape.42
  171.2 0.3 select_reduce_fusion
  171.5 0.1 fusion.5
  171.6 0.6 pad.4.clone
  172.2 19.5 %shard_map.86 = f32[8,128]{1,0:T(8,128)} custom-call(f32[4,2,2,8,128]{4,3,2,1,0:T(8,128)} %bitcast.36), custom_call_target="tpu_custom_call" | custom-call | tf_op jit(solution)/shard_map/pallas_call | solution.py:507
  191.7 0.7 slice_reduce_fusion
  192.4 0.0 copy-done.2
  192.5 1.3 bitcast_subtract_fusion
  193.7 12.2 %fusion = bf16[2,1024,2880]{1,2,0:T(8,128)(2,1)} fusion(bf16[2,16,32,2880]{3,2,1,0:T(8,128)(2,1)} %get-tuple-element.11, bf16[2,16,32,1024]{3,2,1,0:T(8,128)(2,1)} %param.5), kind=kOutput, calls=%fused_computation.1 | convolution fusion | flops 6045696000 | bytes 19791872 | tf_op jit(solution)/shard_map/escj,escd->ejd/dot_general | solution.py:576
  206.0 0.0 copy-done
  206.0 1.3 copy.75
  (11 shorter events, 0.1 us)
Async XLA Ops:
  17.9 4.1 %copy-start.1 = (bf16[16,64,128]{2,1,0:T(8,128)(2,1)}, bf16[16,64,128]{2,1,0:T(8,128)(2,1)S(1)}, u32[]{:S(2)}) copy-start(bf16[16,64,128]{2,1,0:T(8,128)(2,1)S(1)} %fusion.3.select_ref) | copy-start | bytes 786436
  22.0 170.5 %copy-start.2 = (f32[128,4]{0,1:T(4,128)S(1)}, f32[128,4]{0,1:T(4,128)}, u32[]{:S(2)}) copy-start(f32[128,4]{0,1:T(4,128)} %param.8) | copy-start | bytes 6148
  193.7 12.2 %copy-start = (bf16[2,512,1024]{2,1,0:T(8,128)(2,1)S(1)}, bf16[2,512,1024]{2,1,0:T(8,128)(2,1)}, u32[]{:S(2)}) copy-start(bf16[2,512,1024]{2,1,0:T(8,128)(2,1)} %get-tuple-element.10) | copy-start | bytes 6291460

commit v4 on v3

--- a/solution.py
+++ b/solution.py
@@ -227,7 +227,6 @@
         lax.fori_loop(0, PAIR, lambda xi, _: (mix(zi, xi, 1 - c, put_away), 0)[1], 0)
         rc(i).start()
         lax.fori_loop(0, PAIR, lambda xi, _: (mix(zi, xi, c, put_home), 0)[1], 0)
-        gather_core(i)
 
     def add(first, others):
         total = first.astype(F32)
@@ -277,6 +276,8 @@
 
     for i in range(outer):
         sum_core(i)
+    for k in range(outer):
+        gather_core(k)
     for h in range(2):
         for k in range(outer):
             gc(h, k).wait_recv()

time: 208 us -> 205 us (0.986)
  Pallas kernels: 178 us -> 175 us
    pallas_call x1, Pallas kernels: 146 us -> 141 us  [exchange(): pl.pallas_call(functools.partial(exchange_kernel, outer, parts), out_shap...]
where the time goes in v4:
time: 205 us; the launch traced here: 204 us
  Pallas kernels  175 us (85%)
  matrix products  12.4 us (6%)
  local copies, waits for them, and re-layouts  9.14 us (4%)
  other arithmetic  6.85 us (3%)
    pallas_call x1, Pallas kernels, exchange(): pl.pallas_call(functools.partial(exchange_kernel, outer, parts), out_shap...  141 us
    pallas_call x1, Pallas kernels, total_routes(): pl.pallas_call(functools.partial(total_kernel, outer, parts), out_shape=j...  21.2 us
    pallas_call x1, Pallas kernels, gather_routes(): pl.pallas_call(functools.partial(routes_kernel, outer), out_shape=jax.Sha...  12.7 us
    dot_general x1, matrix products, local(): jnp.einsum('escj,escd->ejd', hidden_acts, slot_grad, preferred_element_ty...  12.2 us
    unnamed x10, local copies, waits for them, and re-layouts  5.27 us

profile of v4, /device:TPU:0, one launch (start us, length us, event | category | flops | bytes accessed | tf_op | source)
XLA Modules:
  0.0 204.4 jit_solution(14420649490739373426)
XLA Ops:
  0.6 0.7 exponential_reduce_fusion
  1.4 0.1 eq.45
  1.4 0.7 exponential_divide_fusion
  2.1 0.7 convert_element_type.23
  2.8 0.6 maximum_bitcast_fusion.mine_ref
  3.4 12.7 %shard_map.84 = f32[4,2,2,8,128]{4,3,2,1,0:T(8,128)} custom-call(f32[8,128]{1,0:T(8,128)} %maximum_bitcast_fusion.mine_ref), custom_call_target="tpu_custom_call" | custom-call | tf_op jit(solution)/shard_map/pallas_call | solution.py:451
  16.2 0.9 fusion.8
  17.1 0.1 compare_reduce_fusion
  17.2 0.1 convolution_convert_fusion
  17.4 0.1 fusion.4
  17.5 0.3 select_reduce_fusion.1
  17.7 0.2 fusion.3.select_ref
  17.9 0.0 copy-start.1
  17.9 2.0 copy.63.grad_ref
  19.9 1.1 copy.61.prob_ref
  21.0 1.0 copy.62.back_ref
  22.0 0.0 copy-done.1
  22.0 0.0 copy-start.2
  22.0 141.4 %shard_map.85 = (bf16[4,2,2,2,128,1440]{5,4,3,2,1,0:T(8,128)(2,1)}, bf16[128,1440]{1,0:T(8,128)(2,1)}, bf16[2,512,1024]{2,1,0:T(8,128)(2,1)}, bf16[2,16,32,2880]{3,2,1,0:T(8,128)(2,1)}, f32[2,512,1]{2,1,0:T(8,128)}) custom-call(bf16[2,512,1024]{2,1,0:T(8,128)(2,1)} %bitcast.40, bf16[2,2880,1024]{2,1,0:T(8,128)(2,1)} %bitcast.39, ...), custom_call_target="tpu_custom_call" | custom-call | flops 12079595520 | bytes 23592960 | tf_op jit(solution)/shard_map/pallas_call | solution.py:382
  163.4 1.9 copy.67
  165.3 1.2 reduce.1
  166.5 0.1 reshape.42
  166.6 0.3 select_reduce_fusion
  166.9 0.1 fusion.5
  167.0 0.6 pad.4.clone
  167.7 21.2 %shard_map.86 = f32[8,128]{1,0:T(8,128)} custom-call(f32[4,2,2,8,128]{4,3,2,1,0:T(8,128)} %bitcast.36), custom_call_target="tpu_custom_call" | custom-call | tf_op jit(solution)/shard_map/pallas_call | solution.py:508
  188.9 0.7 slice_reduce_fusion
  189.6 0.0 copy-done.2
  189.6 1.3 bitcast_subtract_fusion
  190.8 12.2 %fusion = bf16[2,1024,2880]{1,2,0:T(8,128)(2,1)} fusion(bf16[2,16,32,2880]{3,2,1,0:T(8,128)(2,1)} %get-tuple-element.11, bf16[2,16,32,1024]{3,2,1,0:T(8,128)(2,1)} %param.5), kind=kOutput, calls=%fused_computation.1 | convolution fusion | flops 6045696000 | bytes 19791872 | tf_op jit(solution)/shard_map/escj,escd->ejd/dot_general | solution.py:577
  203.1 0.0 copy-done
  203.1 1.3 copy.75
  (11 shorter events, 0.1 us)
Async XLA Ops:
  17.9 4.1 %copy-start.1 = (bf16[16,64,128]{2,1,0:T(8,128)(2,1)}, bf16[16,64,128]{2,1,0:T(8,128)(2,1)S(1)}, u32[]{:S(2)}) copy-start(bf16[16,64,128]{2,1,0:T(8,128)(2,1)S(1)} %fusion.3.select_ref) | copy-start | bytes 786436
  22.0 167.6 %copy-start.2 = (f32[128,4]{0,1:T(4,128)S(1)}, f32[128,4]{0,1:T(4,128)}, u32[]{:S(2)}) copy-start(f32[128,4]{0,1:T(4,128)} %param.8) | copy-start | bytes 6148
  190.8 12.2 %copy-start = (bf16[2,512,1024]{2,1,0:T(8,128)(2,1)S(1)}, bf16[2,512,1024]{2,1,0:T(8,128)(2,1)}, u32[]{:S(2)}) copy-start(bf16[2,512,1024]{2,1,0:T(8,128)(2,1)} %get-tuple-element.10) | copy-start | bytes 6291460
